TPU v7x, 32 devices: a whole 2x2x4 slice. The times are simulated.
32 devices in a mesh: cd: 8 (over z, y), ab: 4 (over x, core).
Axes of the slice: x: 2, y: 2, z: 4, core: 2. Of those that a mesh axis runs over, the one named last changes fastest.
Arguments:
- amplitudes: float32 [2, 128, 57344], P(None, 'ab', 'cd'), may hold values from -6 to 6
- integrals: float32 [57344, 1536], P('cd', 'ab'), may hold values from -0.0234375 to 0.0234375
- c_index: int32 [57344], P('cd'), may hold values from 0 to 1532, as said below
- d_index: int32 [57344], P('cd'), may hold values from 0 to 1535
- a_index: int32 [1536], P('ab'), may hold values from 0 to 1532, as said below
- b_index: int32 [1536], P('ab'), may hold values from 0 to 1535
Outputs:
- ladder: float32 [128, 2, 1536], P('cd', None, 'ab')
Inputs may be any that keep to these rules, and one draw needn't show every extreme that they name: c_index[p] <= d_index[p] for every pair; some pairs have c_index equal to d_index. a_index[q] <= b_index[q] for every result pair; some have a_index equal to b_index.
All inputs are finite; a program needn't handle non-finite values.
Results may differ from a plain program's by a relative error of at most 0.00007.
Values sent between devices are 32-bit elements; how exact they have to be, the bound alone decides.
A program may use at most 64 MiB of HBM per device.

v0:
```python
import functools

import jax
import jax.numpy as jnp
from jax import lax
from jax.experimental import pallas as pl
from jax.experimental.pallas import tpu as pltpu
from jax.sharding import PartitionSpec as P

MESH = pl.DeviceIdType.MESH
BF16 = jnp.bfloat16
F32 = jnp.float32

LAST = 8
DEPTH = 1024


def split(x):
    high = x.astype(BF16)
    return high, (x - high.astype(F32)).astype(BF16)


def kernel(n, a_hbm, v_hbm, c_ref, d_ref, qa_ref, qb_ref, out_ref,
           held, v, v_split, weights, total, near, part, recv,
           own_sem, v_sem, cs, cr, xs, xr, fs, fr, rs, rr):
    me = lax.axis_index("cd")
    j = lax.axis_index("ab")
    beside = j + 1 - 2 * lax.rem(j, 2)
    across = lax.rem(j + 2, 4)
    far = lax.rem(beside + 2, 4)
    block = a_hbm.shape[1]
    depth = a_hbm.shape[2]
    pieces = depth // DEPTH
    q = out_ref.shape[2]
    chunks = ((0, block - LAST), (block - LAST, LAST))
    unit = part.shape[2]
    mine = recv.shape[1]

    own = pltpu.make_async_copy(a_hbm, held.at[0], own_sem)
    own.start()

    def v_copy(k):
        at = pl.ds(pl.multiple_of(k * DEPTH, DEPTH), DEPTH)
        return pltpu.make_async_copy(v_hbm.at[at], v.at[at], v_sem.at[k])

    @pl.loop(0, pieces)
    def _(k):
        v_copy(k).start()

    barrier = pltpu.get_barrier_semaphore()
    for other in (beside, across):
        pl.semaphore_signal(barrier, inc=1, device_id={"ab": other}, device_id_type=MESH)

    @pl.loop(1, n)
    def _(step):
        pl.semaphore_signal(
            barrier, inc=1, device_id={"cd": lax.rem(me + step, n)}, device_id_type=MESH
        )

    pl.semaphore_wait(barrier, n + 1)

    def columns(k):
        return pl.ds(pl.multiple_of(k * DEPTH, DEPTH), DEPTH)

    def window(chunk, k):
        return pl.ds(*chunks[chunk]), columns(k)

    def cross_copy(chunk, k):
        rows, cols = window(chunk, k)
        return pltpu.make_async_remote_copy(
            src_ref=a_hbm.at[:, rows, cols], dst_ref=held.at[2, :, rows, cols],
            send_sem=xs.at[chunk, k], recv_sem=xr.at[chunk, k],
            device_id={"ab": across}, device_id_type=MESH,
        )

    def pass_copy(chunk, k):
        rows, cols = window(chunk, k)
        return pltpu.make_async_remote_copy(
            src_ref=held.at[2, :, rows, cols], dst_ref=held.at[3, :, rows, cols],
            send_sem=fs.at[chunk, k], recv_sem=fr.at[chunk, k],
            device_id={"ab": beside}, device_id_type=MESH,
        )

    def near_copy(k):
        cols = columns(k)
        return pltpu.make_async_remote_copy(
            src_ref=a_hbm.at[:, :, cols], dst_ref=held.at[1, :, :, cols],
            send_sem=cs.at[k], recv_sem=cr.at[k],
            device_id={"ab": beside}, device_id_type=MESH,
        )

    @pl.loop(0, pieces)
    def _(k):
        cross_copy(0, k).start()

    @pl.loop(0, pieces)
    def _(k):
        near_copy(k).start()

    same = c_ref[...] == d_ref[...]
    weights[0:1, :] = jnp.where(same, F32(0.5), F32(1.0))
    weights[1:2, :] = jnp.where(same, F32(0.0), F32(1.0))

    def product(first, second, rows, cols):
        plus, minus = weights[0:1, cols], weights[1:2, cols]
        x = jnp.concatenate([
            held[first, 0, rows, cols] * plus, held[first, 1, rows, cols] * minus,
            held[second, 0, rows, cols] * plus, held[second, 1, rows, cols] * minus,
        ], axis=0)
        high, low = split(x)
        count = x.shape[0]
        out = jnp.dot(jnp.concatenate([high, low], axis=0), v_split[cols, :],
                      preferred_element_type=F32)
        return out[:count, :q] + (out[count:, :q] + out[:count, q:])

    def send_sums(row, sums):
        for m in range(8 // unit):
            message = row // unit + m
            for s in range(2):
                part[message, s] = sums[s][m * unit:(m + 1) * unit]
            owner = message // mine

            @pl.when(owner != me)
            def _():
                pltpu.make_async_remote_copy(
                    src_ref=part.at[message],
                    dst_ref=recv.at[lax.rem(me - owner - 1 + n, n), lax.rem(message, mine)],
                    send_sem=rs, recv_sem=rr,
                    device_id={"cd": owner}, device_id_type=MESH,
                ).start()

    own.wait()
    near[...] = jnp.zeros_like(near)

    @pl.loop(0, pieces)
    def _(k):
        cols = columns(k)
        v_copy(k).wait()
        v_split[cols, :q], v_split[cols, q:] = split(v[cols, :])
        near_copy(k).wait_recv()
        near[...] += product(0, 1, pl.ds(0, block), cols)

    for at, owner in ((0, j), (1, beside)):
        for row in range(0, block, 8):
            base = at * 2 * block + row
            send_sums(owner * block + row,
                      [near[base + s * block:base + s * block + 8, :] for s in range(2)])

    for chunk, (start, count) in enumerate(chunks):
        size = 4 * count
        total[:size, :] = jnp.zeros((size, q), F32)

        def add(k):
            rows, cols = window(chunk, k)
            pass_copy(chunk, k).wait_recv()
            total[:size, :] += product(2, 3, rows, cols)

        @pl.loop(0, pieces)
        def _(k):
            cross_copy(chunk, k).wait_recv()
            pass_copy(chunk, k).start()
            cross_copy(chunk, k).wait_send()
            if chunk == 0:
                cross_copy(1, k).start()

            @pl.when(k > 0)
            def _():
                add(k - 1)

        add(pieces - 1)
        for at, owner in ((0, across), (1, far)):
            for row in range(0, count, 8):
                base = at * 2 * count + row
                send_sums(owner * block + start + row,
                          [total[base + s * count:base + s * count + 8, :] for s in range(2)])

    keep = jnp.where(qa_ref[...] == qb_ref[...], F32(0.0), F32(0.5)).reshape(1, q)
    pltpu.make_async_copy(recv, recv, rr).wait()
    for m in range(mine):
        sums = part[me * mine + m]
        sums = lax.fori_loop(0, n - 1, lambda k, acc: acc + recv[k, m], sums)
        out_ref[0, m * unit:(m + 1) * unit, :] = sums[0] * F32(0.5)
        out_ref[1, m * unit:(m + 1) * unit, :] = sums[1] * keep

    pltpu.make_async_copy(recv, recv, rs).wait()

    @pl.loop(0, pieces)
    def _(k):
        near_copy(k).wait_send()

    for chunk in range(2):
        @pl.loop(0, pieces)
        def _(k):
            pass_copy(chunk, k).wait_send()


def local(n, amplitudes, integrals, c_index, d_index, a_index, b_index):
    _, block, depth = amplitudes.shape
    q = integrals.shape[1]
    rows = 4 * block // n
    unit = min(8, rows)
    pieces = depth // DEPTH
    dma = pltpu.SemaphoreType.DMA
    whole = pl.BlockSpec(memory_space=pltpu.VMEM)
    out = pl.pallas_call(
        functools.partial(kernel, n),
        out_shape=jax.ShapeDtypeStruct((2, rows, q), F32),
        in_specs=[pl.BlockSpec(memory_space=pl.ANY)] * 2 + [whole] * 4,
        out_specs=whole,
        scratch_shapes=[
            pltpu.VMEM((4, 2, block, depth), F32),
            pltpu.VMEM((depth, q), F32),
            pltpu.VMEM((depth, 2 * q), BF16),
            pltpu.VMEM((2, depth), F32),
            pltpu.VMEM((4 * (block - LAST), q), F32),
            pltpu.VMEM((4 * block, q), F32),
            pltpu.VMEM((4 * block // unit, 2, unit, q), F32),
            pltpu.VMEM((n - 1, rows // unit, 2, unit, q), F32),
            dma, dma((pieces,)), dma((pieces,)), dma((pieces,)),
            dma((2, pieces)), dma((2, pieces)), dma((2, pieces)), dma((2, pieces)), dma, dma,
        ],
        compiler_params=pltpu.CompilerParams(
            collective_id=0, has_side_effects=True, vmem_limit_bytes=56 * 1024 * 1024
        ),
        cost_estimate=pl.CostEstimate(
            flops=3 * 2 * 8 * block * depth * q,
            bytes_accessed=4 * depth * (q + 2 * block), transcendentals=0,
        ),
    )(amplitudes, integrals, c_index.reshape(1, -1), d_index.reshape(1, -1),
      a_index, b_index)
    return jnp.transpose(out, (1, 0, 2))


def solution(mesh):
    placed = (P(None, "ab", "cd"), P("cd", "ab"), P("cd"), P("cd"), P("ab"), P("ab"))
    return jax.shard_map(
        functools.partial(local, mesh.shape["cd"]), mesh=mesh, in_specs=placed,
        out_specs=P("cd", None, "ab"), check_vma=False,
    )
```

profile of v0, /device:TPU:0, one launch (start us, length us, event | category | flops | bytes accessed | tf_op | source)
XLA Modules:
  0.0 54.2 jit_solution(5970749578125793190)
XLA Ops:
  0.0 52.8 %shard_map.64 = f32[2,16,384]{2,1,0:T(8,128)} custom-call(f32[2,32,7168]{2,1,0:T(8,128)} %a_hbm.1, f32[7168,384]{1,0:T(8,128)} %v_hbm.1, s32[1,7168]{1,0:T(1,128)} %bitcast.4, s32[1,7168]{1,0:T(1,128)} %bitcast.5, s32[384]{0:T(512)} %qa_ref.1, s32[384]{0:T(512)} %qb_ref.1), custom_call_target="tpu_custom_call" | custom-call | flops 4227858432 | bytes 12845056 | tf_op jit(solution)/shard_map/pallas_call | solution.py:205
  52.8 1.4 %copy.7 = f32[16,2,384]{2,1,0:T(2,128)} copy(f32[16,2,384]{2,0,1:T(8,128)} %bitcast.3) | data formatting | bytes 98304 | tf_op jit(solution)/shard_map/transpose | solution.py:231
where the time goes:
time: 54.4 us; the launch traced here: 54.2 us
  Pallas kernels  52.8 us (97%)
  local copies, waits for them, and re-layouts  1.44 us (3%)
    pallas_call x1, Pallas kernels, local(): pl.pallas_call(functools.partial(kernel, n), out_shape=jax.ShapeDtypeStru...  52.8 us
    transpose x1, local copies, waits for them, and re-layouts, local(): return jnp.transpose(out, (1, 0, 2))  1.44 us

commit v1 on v0

v1 whole, which is shorter than its diff:
```python
import functools

import jax
import jax.numpy as jnp
from jax import lax
from jax.experimental import pallas as pl
from jax.experimental.pallas import tpu as pltpu
from jax.sharding import PartitionSpec as P

MESH = pl.DeviceIdType.MESH
BF16 = jnp.bfloat16
F32 = jnp.float32

LAST = 8
DEPTH = 1024


def split(x):
    high = x.astype(BF16)
    return high, (x - high.astype(F32)).astype(BF16)


def kernel(n, a_hbm, v_hbm, c_hbm, d_hbm, qa_hbm, qb_hbm, out_ref,
           held, v, v_split, weights, c_ref, d_ref, qa_ref, qb_ref, total, near, part, recv,
           own_sem, v_sem, index_sem, cs, cr, xs, xr, fs, fr, rs, rr):
    me = lax.axis_index("cd")
    j = lax.axis_index("ab")
    beside = j + 1 - 2 * lax.rem(j, 2)
    across = lax.rem(j + 2, 4)
    far = lax.rem(beside + 2, 4)
    block = a_hbm.shape[1]
    depth = a_hbm.shape[2]
    pieces = depth // DEPTH
    q = out_ref.shape[2]
    chunks = ((0, 2, block - LAST), (0, 1, LAST), (1, 1, LAST))

    def first_row(chunk, parity):
        return LAST * (1 - parity) if chunk == 0 else (block - LAST) * parity

    unit = part.shape[2]
    mine = recv.shape[1]

    barrier = pltpu.get_barrier_semaphore()
    for other in (beside, across):
        pl.semaphore_signal(barrier, inc=1, device_id={"ab": other}, device_id_type=MESH)

    @pl.loop(1, n)
    def _(step):
        pl.semaphore_signal(
            barrier, inc=1, device_id={"cd": lax.rem(me + step, n)}, device_id_type=MESH
        )

    own = pltpu.make_async_copy(a_hbm, held.at[0], own_sem)
    own.start()

    def v_copy(k):
        at = pl.ds(pl.multiple_of(k * DEPTH, DEPTH), DEPTH)
        return pltpu.make_async_copy(v_hbm.at[at], v.at[at], v_sem.at[k])

    @pl.loop(0, pieces)
    def _(k):
        v_copy(k).start()

    pl.semaphore_wait(barrier, n + 1)

    def columns(k):
        return pl.ds(pl.multiple_of(k * DEPTH, DEPTH), DEPTH)

    parity = lax.rem(j, 2)

    def window(chunk, k):
        slab, slabs, count = chunks[chunk]
        row = pl.multiple_of(first_row(chunk, parity), 8)
        return pl.ds(slab, slabs), pl.ds(row, count), columns(k)

    def cross_copy(chunk, k):
        at = window(chunk, k)
        return pltpu.make_async_remote_copy(
            src_ref=a_hbm.at[*at], dst_ref=held.at[2, *at],
            send_sem=xs.at[chunk, k], recv_sem=xr.at[chunk, k],
            device_id={"ab": across}, device_id_type=MESH,
        )

    def pass_copy(chunk, k):
        at = window(chunk, k)
        return pltpu.make_async_remote_copy(
            src_ref=held.at[2, *at], dst_ref=held.at[3, *at],
            send_sem=fs.at[chunk, k], recv_sem=fr.at[chunk, k],
            device_id={"ab": beside}, device_id_type=MESH,
        )

    def near_copy(k):
        cols = columns(k)
        return pltpu.make_async_remote_copy(
            src_ref=a_hbm.at[:, :, cols], dst_ref=held.at[1, :, :, cols],
            send_sem=cs.at[k], recv_sem=cr.at[k],
            device_id={"ab": beside}, device_id_type=MESH,
        )

    @pl.loop(0, pieces)
    def _(k):
        cross_copy(0, k).start()

    @pl.loop(0, pieces)
    def _(k):
        near_copy(k).start()

    index_copies = [
        pltpu.make_async_copy(src, dst, index_sem.at[i])
        for i, (src, dst) in enumerate(
            ((c_hbm, c_ref), (d_hbm, d_ref), (qa_hbm, qa_ref), (qb_hbm, qb_ref)))
    ]
    for copy in index_copies:
        copy.start()
    for copy in index_copies:
        copy.wait()
    same = c_ref[...] == d_ref[...]
    weights[0:1, :] = jnp.where(same, F32(0.5), F32(1.0))
    weights[1:2, :] = jnp.where(same, F32(0.0), F32(1.0))

    def product(cols, *operands):
        x = jnp.concatenate([
            held[slot, slab, rows, cols] * weights[slab:slab + 1, cols]
            for slot, slab, rows in operands
        ], axis=0)
        high, low = split(x)
        count = x.shape[0]
        out = jnp.dot(jnp.concatenate([high, low], axis=0), v_split[cols, :],
                      preferred_element_type=F32)
        return out[:count, :q] + (out[count:, :q] + out[:count, q:])

    def send_sums(row, sums):
        slabs = pl.ds(min(sums), len(sums))
        for m in range(8 // unit):
            message = row // unit + m
            for slab, value in sums.items():
                part[message, slab] = value[m * unit:(m + 1) * unit]
            owner = message // mine

            @pl.when(owner != me)
            def _():
                pltpu.make_async_remote_copy(
                    src_ref=part.at[message, slabs],
                    dst_ref=recv.at[lax.rem(me - owner - 1 + n, n), lax.rem(message, mine), slabs],
                    send_sem=rs, recv_sem=rr,
                    device_id={"cd": owner}, device_id_type=MESH,
                ).start()

    own.wait()
    near[...] = jnp.zeros_like(near)

    @pl.loop(0, pieces)
    def _(k):
        cols = columns(k)
        v_copy(k).wait()
        v_split[cols, :q], v_split[cols, q:] = split(v[cols, :])
        near_copy(k).wait_recv()
        near[...] += product(
            cols, *((slot, slab, pl.ds(0, block)) for slot in (0, 1) for slab in range(2)))

    for at, owner in ((0, j), (1, beside)):
        for row in range(0, block, 8):
            base = at * 2 * block + row
            send_sums(owner * block + row,
                      {s: near[base + s * block:base + s * block + 8, :] for s in range(2)})

    for chunk, (slab, slabs, count) in enumerate(chunks):
        blocks = ((2, across, parity), (3, far, 1 - parity))
        size = 2 * slabs * count
        total[:size, :] = jnp.zeros((size, q), F32)

        def add(k):
            pass_copy(chunk, k).wait_recv()
            total[:size, :] += product(columns(k), *(
                (slot, one, pl.ds(pl.multiple_of(first_row(chunk, odd), 8), count))
                for slot, _, odd in blocks for one in range(slab, slab + slabs)))

        @pl.loop(0, pieces)
        def _(k):
            cross_copy(chunk, k).wait_recv()
            pass_copy(chunk, k).start()
            cross_copy(chunk, k).wait_send()
            if chunk + 1 < len(chunks):
                cross_copy(chunk + 1, k).start()

            @pl.when(k > 0)
            def _():
                add(k - 1)

        add(pieces - 1)
        for at, (_, owner, odd) in enumerate(blocks):
            for row in range(0, count, 8):
                base = at * slabs * count + row
                send_sums(owner * block + first_row(chunk, odd) + row, {
                    slab + s: total[base + s * count:base + s * count + 8, :]
                    for s in range(slabs)})

    @pl.loop(0, pieces)
    def _(k):
        near_copy(k).wait_send()
        for chunk in range(len(chunks)):
            pass_copy(chunk, k).wait_send()

    keep = jnp.where(qa_ref[...] == qb_ref[...], F32(0.0), F32(0.5)).reshape(1, q)
    pltpu.make_async_copy(recv, recv, rr).wait()
    for m in range(mine):
        sums = part[me * mine + m]
        sums = lax.fori_loop(0, n - 1, lambda k, acc: acc + recv[k, m], sums)
        out_ref[0, m * unit:(m + 1) * unit, :] = sums[0] * F32(0.5)
        out_ref[1, m * unit:(m + 1) * unit, :] = sums[1] * keep

    pltpu.make_async_copy(recv, recv, rs).wait()


def local(n, amplitudes, integrals, c_index, d_index, a_index, b_index):
    _, block, depth = amplitudes.shape
    q = integrals.shape[1]
    rows = 4 * block // n
    unit = min(8, rows)
    pieces = depth // DEPTH
    dma = pltpu.SemaphoreType.DMA
    out = pl.pallas_call(
        functools.partial(kernel, n),
        out_shape=jax.ShapeDtypeStruct((2, rows, q), F32),
        in_specs=[pl.BlockSpec(memory_space=pl.ANY)] * 6,
        out_specs=pl.BlockSpec(memory_space=pltpu.VMEM),
        scratch_shapes=[
            pltpu.VMEM((4, 2, block, depth), F32),
            pltpu.VMEM((depth, q), F32),
            pltpu.VMEM((depth, 2 * q), BF16),
            pltpu.VMEM((2, depth), F32),
            pltpu.VMEM((1, depth), jnp.int32),
            pltpu.VMEM((1, depth), jnp.int32),
            pltpu.VMEM((q,), jnp.int32),
            pltpu.VMEM((q,), jnp.int32),
            pltpu.VMEM((4 * (block - LAST), q), F32),
            pltpu.VMEM((4 * block, q), F32),
            pltpu.VMEM((4 * block // unit, 2, unit, q), F32),
            pltpu.VMEM((n - 1, rows // unit, 2, unit, q), F32),
            dma, dma((pieces,)), dma((4,)), dma((pieces,)), dma((pieces,)),
            dma((3, pieces)), dma((3, pieces)), dma((3, pieces)), dma((3, pieces)), dma, dma,
        ],
        compiler_params=pltpu.CompilerParams(
            collective_id=0, has_side_effects=True, vmem_limit_bytes=56 * 1024 * 1024
        ),
        cost_estimate=pl.CostEstimate(
            flops=3 * 2 * 8 * block * depth * q,
            bytes_accessed=4 * depth * (q + 2 * block), transcendentals=0,
        ),
    )(amplitudes, integrals, c_index.reshape(1, -1), d_index.reshape(1, -1),
      a_index, b_index)
    return jnp.transpose(out, (1, 0, 2))


def solution(mesh):
    placed = (P(None, "ab", "cd"), P("cd", "ab"), P("cd"), P("cd"), P("ab"), P("ab"))
    return jax.shard_map(
        functools.partial(local, mesh.shape["cd"]), mesh=mesh, in_specs=placed,
        out_specs=P("cd", None, "ab"), check_vma=False,
    )
```

time: 54.4 us -> 55.4 us (1.018)
  the two profiles are of different devices: /device:TPU:0 before, /device:TPU:2 now
where the time goes in v1:
time: 55.4 us; the launch traced here: 54.5 us
  Pallas kernels  53 us (96%)
  local copies, waits for them, and re-layouts  1.44 us (3%)
    pallas_call x1, Pallas kernels, local(): pl.pallas_call(functools.partial(kernel, n), out_shape=jax.ShapeDtypeStru...  53 us
    transpose x1, local copies, waits for them, and re-layouts, local(): return jnp.transpose(out, (1, 0, 2))  1.44 us

profile of v1, /device:TPU:2, one launch (start us, length us, event | category | flops | bytes accessed | tf_op | source)
XLA Modules:
  0.0 54.5 jit_solution(18343650116097861051)
XLA Ops:
  0.0 53.0 %shard_map.64 = f32[2,16,384]{2,1,0:T(8,128)} custom-call(f32[2,32,7168]{2,1,0:T(8,128)} %a_hbm.1, f32[7168,384]{1,0:T(8,128)} %v_hbm.1, s32[1,7168]{1,0:T(1,128)} %bitcast.4, s32[1,7168]{1,0:T(1,128)} %bitcast.5, s32[384]{0:T(512)} %qa_hbm.1, s32[384]{0:T(512)} %qb_hbm.1), custom_call_target="tpu_custom_call" | custom-call | flops 4227858432 | bytes 12845056 | tf_op jit(solution)/shard_map/pallas_call | solution.py:222
  53.0 1.4 %copy.7 = f32[16,2,384]{2,1,0:T(2,128)} copy(f32[16,2,384]{2,0,1:T(8,128)} %bitcast.3) | data formatting | bytes 98304 | tf_op jit(solution)/shard_map/transpose | solution.py:252

commit v2 on v1

--- a/solution.py
+++ b/solution.py
@@ -32,7 +32,7 @@
     depth = a_hbm.shape[2]
     pieces = depth // DEPTH
     q = out_ref.shape[2]
-    chunks = ((0, 2, block - LAST), (0, 1, LAST), (1, 1, LAST))
+    chunks = (block - LAST, LAST)
 
     def first_row(chunk, parity):
         return LAST * (1 - parity) if chunk == 0 else (block - LAST) * parity
@@ -69,9 +69,8 @@
     parity = lax.rem(j, 2)
 
     def window(chunk, k):
-        slab, slabs, count = chunks[chunk]
         row = pl.multiple_of(first_row(chunk, parity), 8)
-        return pl.ds(slab, slabs), pl.ds(row, count), columns(k)
+        return slice(None), pl.ds(row, chunks[chunk]), columns(k)
 
     def cross_copy(chunk, k):
         at = window(chunk, k)
@@ -129,22 +128,25 @@
                       preferred_element_type=F32)
         return out[:count, :q] + (out[count:, :q] + out[:count, q:])
 
-    def send_sums(row, sums):
-        slabs = pl.ds(min(sums), len(sums))
-        for m in range(8 // unit):
-            message = row // unit + m
-            for slab, value in sums.items():
-                part[message, slab] = value[m * unit:(m + 1) * unit]
-            owner = message // mine
-
-            @pl.when(owner != me)
-            def _():
-                pltpu.make_async_remote_copy(
-                    src_ref=part.at[message, slabs],
-                    dst_ref=recv.at[lax.rem(me - owner - 1 + n, n), lax.rem(message, mine), slabs],
-                    send_sem=rs, recv_sem=rr,
-                    device_id={"cd": owner}, device_id_type=MESH,
-                ).start()
+    def send_sums(sums, at, row, count):
+        @pl.loop(0, count, step=8)
+        def _(done):
+            values = [sums[pl.ds(pl.multiple_of(at + s * count + done, 8), 8), :]
+                      for s in range(2)]
+            for m in range(8 // unit):
+                message = (row + done) // unit + m
+                for s in range(2):
+                    part[message, s] = values[s][m * unit:(m + 1) * unit]
+                owner = message // mine
+
+                @pl.when(owner != me)
+                def _():
+                    slot = lax.rem(me - owner - 1 + n, n)
+                    pltpu.make_async_remote_copy(
+                        src_ref=part.at[message], dst_ref=recv.at[slot, lax.rem(message, mine)],
+                        send_sem=rs, recv_sem=rr,
+                        device_id={"cd": owner}, device_id_type=MESH,
+                    ).start()
 
     own.wait()
     near[...] = jnp.zeros_like(near)
@@ -159,29 +161,26 @@
             cols, *((slot, slab, pl.ds(0, block)) for slot in (0, 1) for slab in range(2)))
 
     for at, owner in ((0, j), (1, beside)):
-        for row in range(0, block, 8):
-            base = at * 2 * block + row
-            send_sums(owner * block + row,
-                      {s: near[base + s * block:base + s * block + 8, :] for s in range(2)})
-
-    for chunk, (slab, slabs, count) in enumerate(chunks):
+        send_sums(near, at * 2 * block, owner * block, block)
+
+    for chunk, count in enumerate(chunks):
         blocks = ((2, across, parity), (3, far, 1 - parity))
-        size = 2 * slabs * count
+        size = 4 * count
         total[:size, :] = jnp.zeros((size, q), F32)
 
         def add(k):
             pass_copy(chunk, k).wait_recv()
             total[:size, :] += product(columns(k), *(
-                (slot, one, pl.ds(pl.multiple_of(first_row(chunk, odd), 8), count))
-                for slot, _, odd in blocks for one in range(slab, slab + slabs)))
+                (slot, slab, pl.ds(pl.multiple_of(first_row(chunk, odd), 8), count))
+                for slot, _, odd in blocks for slab in range(2)))
 
         @pl.loop(0, pieces)
         def _(k):
             cross_copy(chunk, k).wait_recv()
             pass_copy(chunk, k).start()
             cross_copy(chunk, k).wait_send()
-            if chunk + 1 < len(chunks):
-                cross_copy(chunk + 1, k).start()
+            if chunk == 0:
+                cross_copy(1, k).start()
 
             @pl.when(k > 0)
             def _():
@@ -189,11 +188,7 @@
 
         add(pieces - 1)
         for at, (_, owner, odd) in enumerate(blocks):
-            for row in range(0, count, 8):
-                base = at * slabs * count + row
-                send_sums(owner * block + first_row(chunk, odd) + row, {
-                    slab + s: total[base + s * count:base + s * count + 8, :]
-                    for s in range(slabs)})
+            send_sums(total, at * 2 * count, owner * block + first_row(chunk, odd), count)
 
     @pl.loop(0, pieces)
     def _(k):
@@ -222,7 +217,7 @@
     out = pl.pallas_call(
         functools.partial(kernel, n),
         out_shape=jax.ShapeDtypeStruct((2, rows, q), F32),
-        in_specs=[pl.BlockSpec(memory_space=pl.ANY)] * 6,
+        in_specs=[pl.BlockSpec(memory_space=pltpu.HBM)] * 6,
         out_specs=pl.BlockSpec(memory_space=pltpu.VMEM),
         scratch_shapes=[
             pltpu.VMEM((4, 2, block, depth), F32),
@@ -238,17 +233,17 @@
             pltpu.VMEM((4 * block // unit, 2, unit, q), F32),
             pltpu.VMEM((n - 1, rows // unit, 2, unit, q), F32),
             dma, dma((pieces,)), dma((4,)), dma((pieces,)), dma((pieces,)),
-            dma((3, pieces)), dma((3, pieces)), dma((3, pieces)), dma((3, pieces)), dma, dma,
+            dma((2, pieces)), dma((2, pieces)), dma((2, pieces)), dma((2, pieces)), dma, dma,
         ],
         compiler_params=pltpu.CompilerParams(
-            collective_id=0, has_side_effects=True, vmem_limit_bytes=56 * 1024 * 1024
+            collective_id=0, has_side_effects=True, vmem_limit_bytes=44 * 1024 * 1024
         ),
         cost_estimate=pl.CostEstimate(
             flops=3 * 2 * 8 * block * depth * q,
             bytes_accessed=4 * depth * (q + 2 * block), transcendentals=0,
         ),
-    )(amplitudes, integrals, c_index.reshape(1, -1), d_index.reshape(1, -1),
-      a_index, b_index)
+    )(*(pltpu.with_memory_space_constraint(x, pltpu.HBM) for x in (
+        amplitudes, integrals, c_index.reshape(1, -1), d_index.reshape(1, -1), a_index, b_index)))
     return jnp.transpose(out, (1, 0, 2))
 
 

time: 55.4 us -> 52.1 us (0.940)
  Pallas kernels: 53 us -> 51 us
  local copies, waits for them, and re-layouts: 1.44 us -> 0.65 us
    pallas_call x1, Pallas kernels: 53 us -> 51 us  [local(): pl.pallas_call(functools.partial(kernel, n), out_shape=jax.ShapeDtypeStru...]
    transpose x1, local copies, waits for them, and re-layouts: 1.44 us -> 0.65 us  [local(): return jnp.transpose(out, (1, 0, 2))]
where the time goes in v2:
time: 52.1 us; the launch traced here: 51.7 us
  Pallas kernels  51 us (98%)
  local copies, waits for them, and re-layouts  0.65 us (1%)
    pallas_call x1, Pallas kernels, local(): pl.pallas_call(functools.partial(kernel, n), out_shape=jax.ShapeDtypeStru...  51 us

profile of v2, /device:TPU:2, one launch (start us, length us, event | category | flops | bytes accessed | tf_op | source)
XLA Modules:
  0.0 51.7 jit_solution(12365893687951519912)
XLA Ops:
  0.0 51.0 %shard_map.64 = f32[2,16,384]{2,1,0:T(8,128)S(1)} custom-call(f32[2,32,7168]{2,1,0:T(8,128)} %a_hbm.1, f32[7168,384]{1,0:T(8,128)} %v_hbm.1, s32[1,7168]{1,0:T(1,128)} %bitcast.4, s32[1,7168]{1,0:T(1,128)} %bitcast.5, s32[384]{0:T(512)} %qa_hbm.1, s32[384]{0:T(512)} %qb_hbm.1), custom_call_target="tpu_custom_call" | custom-call | flops 4227858432 | bytes 12845056 | tf_op jit(solution)/shard_map/pallas_call | solution.py:217
  51.0 0.6 %copy.7 = f32[16,2,384]{2,1,0:T(2,128)} copy(f32[16,2,384]{2,0,1:T(8,128)S(1)} %bitcast.3) | data formatting | bytes 98304 | tf_op jit(solution)/shard_map/transpose | solution.py:247

commit v3 on v2

--- a/solution.py
+++ b/solution.py
@@ -32,10 +32,12 @@
     depth = a_hbm.shape[2]
     pieces = depth // DEPTH
     q = out_ref.shape[2]
-    chunks = (block - LAST, LAST)
-
-    def first_row(chunk, parity):
-        return LAST * (1 - parity) if chunk == 0 else (block - LAST) * parity
+    groups = ((0, 2, block - LAST), (0, 1, LAST), (1, 1, LAST))
+    chunks = ((0, 1), (2,))
+
+    def first_row(group, parity):
+        row = LAST * (1 - parity) if group == 0 else (block - LAST) * parity
+        return pl.multiple_of(row, 8)
 
     unit = part.shape[2]
     mine = recv.shape[1]
@@ -68,23 +70,23 @@
 
     parity = lax.rem(j, 2)
 
-    def window(chunk, k):
-        row = pl.multiple_of(first_row(chunk, parity), 8)
-        return slice(None), pl.ds(row, chunks[chunk]), columns(k)
-
-    def cross_copy(chunk, k):
-        at = window(chunk, k)
+    def window(group, k):
+        slab, slabs, count = groups[group]
+        return pl.ds(slab, slabs), pl.ds(first_row(group, parity), count), columns(k)
+
+    def cross_copy(group, k):
+        at = window(group, k)
         return pltpu.make_async_remote_copy(
             src_ref=a_hbm.at[*at], dst_ref=held.at[2, *at],
-            send_sem=xs.at[chunk, k], recv_sem=xr.at[chunk, k],
+            send_sem=xs.at[group, k], recv_sem=xr.at[group, k],
             device_id={"ab": across}, device_id_type=MESH,
         )
 
-    def pass_copy(chunk, k):
-        at = window(chunk, k)
+    def pass_copy(group, k):
+        at = window(group, k)
         return pltpu.make_async_remote_copy(
             src_ref=held.at[2, *at], dst_ref=held.at[3, *at],
-            send_sem=fs.at[chunk, k], recv_sem=fr.at[chunk, k],
+            send_sem=fs.at[group, k], recv_sem=fr.at[group, k],
             device_id={"ab": beside}, device_id_type=MESH,
         )
 
@@ -98,7 +100,8 @@
 
     @pl.loop(0, pieces)
     def _(k):
-        cross_copy(0, k).start()
+        for group in chunks[0]:
+            cross_copy(group, k).start()
 
     @pl.loop(0, pieces)
     def _(k):
@@ -128,22 +131,25 @@
                       preferred_element_type=F32)
         return out[:count, :q] + (out[count:, :q] + out[:count, q:])
 
-    def send_sums(sums, at, row, count):
+    def send_sums(sums, at, row, slab, slabs, count):
+        these = pl.ds(slab, slabs)
+
         @pl.loop(0, count, step=8)
         def _(done):
             values = [sums[pl.ds(pl.multiple_of(at + s * count + done, 8), 8), :]
-                      for s in range(2)]
+                      for s in range(slabs)]
             for m in range(8 // unit):
                 message = (row + done) // unit + m
-                for s in range(2):
-                    part[message, s] = values[s][m * unit:(m + 1) * unit]
+                for s in range(slabs):
+                    part[message, slab + s] = values[s][m * unit:(m + 1) * unit]
                 owner = message // mine
 
                 @pl.when(owner != me)
                 def _():
                     slot = lax.rem(me - owner - 1 + n, n)
                     pltpu.make_async_remote_copy(
-                        src_ref=part.at[message], dst_ref=recv.at[slot, lax.rem(message, mine)],
+                        src_ref=part.at[message, these],
+                        dst_ref=recv.at[slot, lax.rem(message, mine), these],
                         send_sem=rs, recv_sem=rr,
                         device_id={"cd": owner}, device_id_type=MESH,
                     ).start()
@@ -161,40 +167,51 @@
             cols, *((slot, slab, pl.ds(0, block)) for slot in (0, 1) for slab in range(2)))
 
     for at, owner in ((0, j), (1, beside)):
-        send_sums(near, at * 2 * block, owner * block, block)
-
-    for chunk, count in enumerate(chunks):
+        send_sums(near, at * 2 * block, owner * block, 0, 2, block)
+
+    for chunk in chunks:
         blocks = ((2, across, parity), (3, far, 1 - parity))
-        size = 4 * count
+        size = sum(2 * groups[group][1] * groups[group][2] for group in chunk)
         total[:size, :] = jnp.zeros((size, q), F32)
 
         def add(k):
-            pass_copy(chunk, k).wait_recv()
+            for group in chunk:
+                pass_copy(group, k).wait_recv()
             total[:size, :] += product(columns(k), *(
-                (slot, slab, pl.ds(pl.multiple_of(first_row(chunk, odd), 8), count))
-                for slot, _, odd in blocks for slab in range(2)))
+                (slot, slab + s, pl.ds(first_row(group, odd), count))
+                for group in chunk for slab, slabs, count in (groups[group],)
+                for slot, _, odd in blocks for s in range(slabs)))
 
         @pl.loop(0, pieces)
         def _(k):
-            cross_copy(chunk, k).wait_recv()
-            pass_copy(chunk, k).start()
-            cross_copy(chunk, k).wait_send()
-            if chunk == 0:
-                cross_copy(1, k).start()
+            for group in chunk:
+                cross_copy(group, k).wait_recv()
+                pass_copy(group, k).start()
+            if chunk == chunks[0]:
+                for group in chunk:
+                    cross_copy(group, k).wait_send()
+                for group in chunks[1]:
+                    cross_copy(group, k).start()
 
             @pl.when(k > 0)
             def _():
                 add(k - 1)
 
         add(pieces - 1)
-        for at, (_, owner, odd) in enumerate(blocks):
-            send_sums(total, at * 2 * count, owner * block + first_row(chunk, odd), count)
+        at = 0
+        for group in chunk:
+            slab, slabs, count = groups[group]
+            for _, owner, odd in blocks:
+                send_sums(total, at, owner * block + first_row(group, odd), slab, slabs, count)
+                at += slabs * count
 
     @pl.loop(0, pieces)
     def _(k):
         near_copy(k).wait_send()
-        for chunk in range(len(chunks)):
-            pass_copy(chunk, k).wait_send()
+        for group in range(len(groups)):
+            pass_copy(group, k).wait_send()
+        for group in chunks[1]:
+            cross_copy(group, k).wait_send()
 
     keep = jnp.where(qa_ref[...] == qb_ref[...], F32(0.0), F32(0.5)).reshape(1, q)
     pltpu.make_async_copy(recv, recv, rr).wait()
@@ -228,12 +245,12 @@
             pltpu.VMEM((1, depth), jnp.int32),
             pltpu.VMEM((q,), jnp.int32),
             pltpu.VMEM((q,), jnp.int32),
-            pltpu.VMEM((4 * (block - LAST), q), F32),
+            pltpu.VMEM((4 * block, q), F32),
             pltpu.VMEM((4 * block, q), F32),
             pltpu.VMEM((4 * block // unit, 2, unit, q), F32),
             pltpu.VMEM((n - 1, rows // unit, 2, unit, q), F32),
             dma, dma((pieces,)), dma((4,)), dma((pieces,)), dma((pieces,)),
-            dma((2, pieces)), dma((2, pieces)), dma((2, pieces)), dma((2, pieces)), dma, dma,
+            dma((3, pieces)), dma((3, pieces)), dma((3, pieces)), dma((3, pieces)), dma, dma,
         ],
         compiler_params=pltpu.CompilerParams(
             collective_id=0, has_side_effects=True, vmem_limit_bytes=44 * 1024 * 1024

time: 52.1 us -> 54.8 us (1.052)
  Pallas kernels: 51 us -> 53.7 us
    pallas_call x1, Pallas kernels: 51 us -> 53.7 us  [local(): pl.pallas_call(functools.partial(kernel, n), out_shape=jax.ShapeDtypeStru...]
where the time goes in v3:
time: 54.8 us; the launch traced here: 54.3 us
  Pallas kernels  53.7 us (98%)
  local copies, waits for them, and re-layouts  0.65 us (1%)
    pallas_call x1, Pallas kernels, local(): pl.pallas_call(functools.partial(kernel, n), out_shape=jax.ShapeDtypeStru...  53.7 us

profile of v3, /device:TPU:2, one launch (start us, length us, event | category | flops | bytes accessed | tf_op | source)
XLA Modules:
  0.0 54.3 jit_solution(7746757396466507031)
XLA Ops:
  0.0 53.7 %shard_map.64 = f32[2,16,384]{2,1,0:T(8,128)S(1)} custom-call(f32[2,32,7168]{2,1,0:T(8,128)} %a_hbm.1, f32[7168,384]{1,0:T(8,128)} %v_hbm.1, s32[1,7168]{1,0:T(1,128)} %bitcast.4, s32[1,7168]{1,0:T(1,128)} %bitcast.5, s32[384]{0:T(512)} %qa_hbm.1, s32[384]{0:T(512)} %qb_hbm.1), custom_call_target="tpu_custom_call" | custom-call | flops 4227858432 | bytes 12845056 | tf_op jit(solution)/shard_map/pallas_call | solution.py:234
  53.7 0.6 %copy.7 = f32[16,2,384]{2,1,0:T(2,128)} copy(f32[16,2,384]{2,0,1:T(8,128)S(1)} %bitcast.3) | data formatting | bytes 98304 | tf_op jit(solution)/shard_map/transpose | solution.py:264

commit v4 on v3

--- a/solution.py
+++ b/solution.py
@@ -13,6 +13,7 @@
 
 LAST = 8
 DEPTH = 1024
+LAG = 1
 
 
 def split(x):
@@ -32,8 +33,8 @@
     depth = a_hbm.shape[2]
     pieces = depth // DEPTH
     q = out_ref.shape[2]
-    groups = ((0, 2, block - LAST), (0, 1, LAST), (1, 1, LAST))
-    chunks = ((0, 1), (2,))
+    groups = ((0, 2, block - LAST), (0, 2, LAST))
+    chunks = ((0,), (1,))
 
     def first_row(group, parity):
         row = LAST * (1 - parity) if group == 0 else (block - LAST) * parity
@@ -169,41 +170,67 @@
     for at, owner in ((0, j), (1, beside)):
         send_sums(near, at * 2 * block, owner * block, 0, 2, block)
 
-    for chunk in chunks:
-        blocks = ((2, across, parity), (3, far, 1 - parity))
+    blocks = ((2, across, parity), (3, far, 1 - parity))
+
+    def forward(chunk, k):
+        for group in chunk:
+            cross_copy(group, k).wait_recv()
+            pass_copy(group, k).start()
+        if chunk == chunks[0]:
+            for group in chunk:
+                cross_copy(group, k).wait_send()
+            for group in chunks[1]:
+                cross_copy(group, k).start()
+
+    def clear(chunk):
         size = sum(2 * groups[group][1] * groups[group][2] for group in chunk)
         total[:size, :] = jnp.zeros((size, q), F32)
 
-        def add(k):
-            for group in chunk:
-                pass_copy(group, k).wait_recv()
-            total[:size, :] += product(columns(k), *(
-                (slot, slab + s, pl.ds(first_row(group, odd), count))
-                for group in chunk for slab, slabs, count in (groups[group],)
-                for slot, _, odd in blocks for s in range(slabs)))
-
-        @pl.loop(0, pieces)
-        def _(k):
-            for group in chunk:
-                cross_copy(group, k).wait_recv()
-                pass_copy(group, k).start()
-            if chunk == chunks[0]:
-                for group in chunk:
-                    cross_copy(group, k).wait_send()
-                for group in chunks[1]:
-                    cross_copy(group, k).start()
-
-            @pl.when(k > 0)
-            def _():
-                add(k - 1)
-
-        add(pieces - 1)
+    def add(chunk, k):
+        for group in chunk:
+            pass_copy(group, k).wait_recv()
+        found = product(columns(k), *(
+            (slot, slab + s, pl.ds(first_row(group, odd), count))
+            for group in chunk for slab, slabs, count in (groups[group],)
+            for slot, _, odd in blocks for s in range(slabs)))
+        total[:found.shape[0], :] += found
+
+    def finish(chunk):
         at = 0
         for group in chunk:
             slab, slabs, count = groups[group]
             for _, owner, odd in blocks:
                 send_sums(total, at, owner * block + first_row(group, odd), slab, slabs, count)
                 at += slabs * count
+
+    clear(chunks[0])
+
+    @pl.loop(0, pieces + LAG)
+    def _(t):
+        @pl.when(t < pieces)
+        def _():
+            forward(chunks[0], t)
+
+        @pl.when(t >= pieces)
+        def _():
+            forward(chunks[1], t - pieces)
+
+        @pl.when(t >= LAG)
+        def _():
+            add(chunks[0], t - LAG)
+
+    finish(chunks[0])
+    clear(chunks[1])
+
+    @pl.loop(LAG, pieces + LAG)
+    def _(t):
+        @pl.when(t < pieces)
+        def _():
+            forward(chunks[1], t)
+
+        add(chunks[1], t - LAG)
+
+    finish(chunks[1])
 
     @pl.loop(0, pieces)
     def _(k):
@@ -250,7 +277,7 @@
             pltpu.VMEM((4 * block // unit, 2, unit, q), F32),
             pltpu.VMEM((n - 1, rows // unit, 2, unit, q), F32),
             dma, dma((pieces,)), dma((4,)), dma((pieces,)), dma((pieces,)),
-            dma((3, pieces)), dma((3, pieces)), dma((3, pieces)), dma((3, pieces)), dma, dma,
+            dma((2, pieces)), dma((2, pieces)), dma((2, pieces)), dma((2, pieces)), dma, dma,
         ],
         compiler_params=pltpu.CompilerParams(
             collective_id=0, has_side_effects=True, vmem_limit_bytes=44 * 1024 * 1024

time: 54.8 us -> 52.2 us (0.953)
  Pallas kernels: 53.7 us -> 51 us
    pallas_call x1, Pallas kernels: 53.7 us -> 51 us  [local(): pl.pallas_call(functools.partial(kernel, n), out_shape=jax.ShapeDtypeStru...]
where the time goes in v4:
time: 52.2 us; the launch traced here: 51.7 us
  Pallas kernels  51 us (98%)
  local copies, waits for them, and re-layouts  0.65 us (1%)
    pallas_call x1, Pallas kernels, local(): pl.pallas_call(functools.partial(kernel, n), out_shape=jax.ShapeDtypeStru...  51 us

profile of v4, /device:TPU:2, one launch (start us, length us, event | category | flops | bytes accessed | tf_op | source)
XLA Modules:
  0.0 51.7 jit_solution(10843122671729757064)
XLA Ops:
  0.0 51.0 %shard_map.64 = f32[2,16,384]{2,1,0:T(8,128)S(1)} custom-call(f32[2,32,7168]{2,1,0:T(8,128)} %a_hbm.1, f32[7168,384]{1,0:T(8,128)} %v_hbm.1, s32[1,7168]{1,0:T(1,128)} %bitcast.4, s32[1,7168]{1,0:T(1,128)} %bitcast.5, s32[384]{0:T(512)} %qa_hbm.1, s32[384]{0:T(512)} %qb_hbm.1), custom_call_target="tpu_custom_call" | custom-call | flops 4227858432 | bytes 12845056 | tf_op jit(solution)/shard_map/pallas_call | solution.py:261
  51.1 0.6 %copy.7 = f32[16,2,384]{2,1,0:T(2,128)} copy(f32[16,2,384]{2,0,1:T(8,128)S(1)} %bitcast.3) | data formatting | bytes 98304 | tf_op jit(solution)/shard_map/transpose | solution.py:291

commit v5 on v4

--- a/solution.py
+++ b/solution.py
@@ -12,7 +12,7 @@
 F32 = jnp.float32
 
 LAST = 8
-DEPTH = 1024
+DEPTH = 1792
 LAG = 1
 
 

time: 52.2 us -> 52.1 us (level)
  no operation moved by 1% of the time
where the time goes in v5:
time: 52.1 us; the launch traced here: 51.6 us
  Pallas kernels  50.9 us (98%)
  local copies, waits for them, and re-layouts  0.65 us (1%)
    pallas_call x1, Pallas kernels, local(): pl.pallas_call(functools.partial(kernel, n), out_shape=jax.ShapeDtypeStru...  50.9 us

profile of v5, /device:TPU:2, one launch (start us, length us, event | category | flops | bytes accessed | tf_op | source)
XLA Modules:
  0.0 51.6 jit_solution(10268593873040905647)
XLA Ops:
  0.0 50.9 %shard_map.64 = f32[2,16,384]{2,1,0:T(8,128)S(1)} custom-call(f32[2,32,7168]{2,1,0:T(8,128)} %a_hbm.1, f32[7168,384]{1,0:T(8,128)} %v_hbm.1, s32[1,7168]{1,0:T(1,128)} %bitcast.4, s32[1,7168]{1,0:T(1,128)} %bitcast.5, s32[384]{0:T(512)} %qa_hbm.1, s32[384]{0:T(512)} %qb_hbm.1), custom_call_target="tpu_custom_call" | custom-call | flops 4227858432 | bytes 12845056 | tf_op jit(solution)/shard_map/pallas_call | solution.py:261
  50.9 0.6 %copy.7 = f32[16,2,384]{2,1,0:T(2,128)} copy(f32[16,2,384]{2,0,1:T(8,128)S(1)} %bitcast.3) | data formatting | bytes 98304 | tf_op jit(solution)/shard_map/transpose | solution.py:291

commit v6 on v4

--- a/solution.py
+++ b/solution.py
@@ -23,7 +23,7 @@
 
 def kernel(n, a_hbm, v_hbm, c_hbm, d_hbm, qa_hbm, qb_hbm, out_ref,
            held, v, v_split, weights, c_ref, d_ref, qa_ref, qb_ref, total, near, part, recv,
-           own_sem, v_sem, index_sem, cs, cr, xs, xr, fs, fr, rs, rr):
+           own_sem, v_sem, index_sem, cs, cr, xs, xr, fs, fr, rs, rr, go_sem, met_sem):
     me = lax.axis_index("cd")
     j = lax.axis_index("ab")
     beside = j + 1 - 2 * lax.rem(j, 2)
@@ -43,15 +43,14 @@
     unit = part.shape[2]
     mine = recv.shape[1]
 
+    first_half = j < 2
+    second_half = j >= 2
     barrier = pltpu.get_barrier_semaphore()
-    for other in (beside, across):
-        pl.semaphore_signal(barrier, inc=1, device_id={"ab": other}, device_id_type=MESH)
-
-    @pl.loop(1, n)
-    def _(step):
-        pl.semaphore_signal(
-            barrier, inc=1, device_id={"cd": lax.rem(me + step, n)}, device_id_type=MESH
-        )
+    pl.semaphore_signal(barrier, inc=1, device_id={"ab": beside}, device_id_type=MESH)
+
+    @pl.when(second_half)
+    def _():
+        pl.semaphore_signal(barrier, inc=1, device_id={"ab": across}, device_id_type=MESH)
 
     own = pltpu.make_async_copy(a_hbm, held.at[0], own_sem)
     own.start()
@@ -64,7 +63,14 @@
     def _(k):
         v_copy(k).start()
 
-    pl.semaphore_wait(barrier, n + 1)
+    @pl.when(first_half)
+    def _():
+        pl.semaphore_wait(barrier, 2)
+        pl.semaphore_signal(go_sem, inc=1, device_id={"ab": across}, device_id_type=MESH)
+
+    @pl.when(second_half)
+    def _():
+        pl.semaphore_wait(go_sem, 1)
 
     def columns(k):
         return pl.ds(pl.multiple_of(k * DEPTH, DEPTH), DEPTH)
@@ -103,6 +109,17 @@
     def _(k):
         for group in chunks[0]:
             cross_copy(group, k).start()
+
+    @pl.when(second_half)
+    def _():
+        @pl.loop(1, n)
+        def _(step):
+            pl.semaphore_signal(
+                barrier, inc=1, device_id={"cd": lax.rem(me + step, n)}, device_id_type=MESH
+            )
+
+        pl.semaphore_wait(barrier, n)
+        pl.semaphore_signal(met_sem, inc=1, device_id={"ab": across}, device_id_type=MESH)
 
     @pl.loop(0, pieces)
     def _(k):
@@ -166,6 +183,10 @@
         near_copy(k).wait_recv()
         near[...] += product(
             cols, *((slot, slab, pl.ds(0, block)) for slot in (0, 1) for slab in range(2)))
+
+    @pl.when(first_half)
+    def _():
+        pl.semaphore_wait(met_sem, 1)
 
     for at, owner in ((0, j), (1, beside)):
         send_sums(near, at * 2 * block, owner * block, 0, 2, block)
@@ -278,6 +299,7 @@
             pltpu.VMEM((n - 1, rows // unit, 2, unit, q), F32),
             dma, dma((pieces,)), dma((4,)), dma((pieces,)), dma((pieces,)),
             dma((2, pieces)), dma((2, pieces)), dma((2, pieces)), dma((2, pieces)), dma, dma,
+            pltpu.SemaphoreType.REGULAR, pltpu.SemaphoreType.REGULAR,
         ],
         compiler_params=pltpu.CompilerParams(
             collective_id=0, has_side_effects=True, vmem_limit_bytes=44 * 1024 * 1024

time: 52.2 us -> 51.6 us (0.989)
  no operation moved by 1% of the time
where the time goes in v6:
time: 51.6 us; the launch traced here: 51.3 us
  Pallas kernels  50.6 us (98%)
  local copies, waits for them, and re-layouts  0.65 us (1%)
    pallas_call x1, Pallas kernels, local(): pl.pallas_call(functools.partial(kernel, n), out_shape=jax.ShapeDtypeStru...  50.6 us

profile of v6, /device:TPU:2, one launch (start us, length us, event | category | flops | bytes accessed | tf_op | source)
XLA Modules:
  0.0 51.3 jit_solution(4724512425979461702)
XLA Ops:
  0.0 50.6 %shard_map.64 = f32[2,16,384]{2,1,0:T(8,128)S(1)} custom-call(f32[2,32,7168]{2,1,0:T(8,128)} %a_hbm.1, f32[7168,384]{1,0:T(8,128)} %v_hbm.1, s32[1,7168]{1,0:T(1,128)} %bitcast.4, s32[1,7168]{1,0:T(1,128)} %bitcast.5, s32[384]{0:T(512)} %qa_hbm.1, s32[384]{0:T(512)} %qb_hbm.1), custom_call_target="tpu_custom_call" | custom-call | flops 4227858432 | bytes 12845056 | tf_op jit(solution)/shard_map/pallas_call | solution.py:282
  50.6 0.6 %copy.7 = f32[16,2,384]{2,1,0:T(2,128)} copy(f32[16,2,384]{2,0,1:T(8,128)S(1)} %bitcast.3) | data formatting | bytes 98304 | tf_op jit(solution)/shard_map/transpose | solution.py:313

commit v7 on v6

--- a/solution.py
+++ b/solution.py
@@ -12,8 +12,8 @@
 F32 = jnp.float32
 
 LAST = 8
-DEPTH = 1024
-LAG = 1
+DEPTH = 1792
+SHORT = 768
 
 
 def split(x):
@@ -77,9 +77,16 @@
 
     parity = lax.rem(j, 2)
 
+    def span(group, k):
+        if group == 1 and isinstance(k, int) and k >= pieces - 1:
+            if k == pieces - 1:
+                return pl.ds(depth - DEPTH, DEPTH - SHORT)
+            return pl.ds(depth - SHORT, SHORT)
+        return columns(k)
+
     def window(group, k):
         slab, slabs, count = groups[group]
-        return pl.ds(slab, slabs), pl.ds(first_row(group, parity), count), columns(k)
+        return pl.ds(slab, slabs), pl.ds(first_row(group, parity), count), span(group, k)
 
     def cross_copy(group, k):
         at = window(group, k)
@@ -200,8 +207,15 @@
         if chunk == chunks[0]:
             for group in chunk:
                 cross_copy(group, k).wait_send()
-            for group in chunks[1]:
-                cross_copy(group, k).start()
+
+            @pl.when(k < pieces - 1)
+            def _():
+                cross_copy(1, k).start()
+
+            @pl.when(k == pieces - 1)
+            def _():
+                cross_copy(1, pieces - 1).start()
+                cross_copy(1, pieces).start()
 
     def clear(chunk):
         size = sum(2 * groups[group][1] * groups[group][2] for group in chunk)
@@ -210,7 +224,7 @@
     def add(chunk, k):
         for group in chunk:
             pass_copy(group, k).wait_recv()
-        found = product(columns(k), *(
+        found = product(span(chunk[0], k), *(
             (slot, slab + s, pl.ds(first_row(group, odd), count))
             for group in chunk for slab, slabs, count in (groups[group],)
             for slot, _, odd in blocks for s in range(slabs)))
@@ -226,7 +240,7 @@
 
     clear(chunks[0])
 
-    @pl.loop(0, pieces + LAG)
+    @pl.loop(0, pieces + 1)
     def _(t):
         @pl.when(t < pieces)
         def _():
@@ -234,32 +248,30 @@
 
         @pl.when(t >= pieces)
         def _():
-            forward(chunks[1], t - pieces)
-
-        @pl.when(t >= LAG)
+            forward(chunks[1], 0)
+
+        @pl.when(t >= 1)
         def _():
-            add(chunks[0], t - LAG)
+            add(chunks[0], t - 1)
 
     finish(chunks[0])
     clear(chunks[1])
 
-    @pl.loop(LAG, pieces + LAG)
-    def _(t):
-        @pl.when(t < pieces)
-        def _():
-            forward(chunks[1], t)
-
-        add(chunks[1], t - LAG)
+    for k in range(1, pieces + 2):
+        if k <= pieces:
+            forward(chunks[1], k)
+        add(chunks[1], k - 1)
 
     finish(chunks[1])
 
     @pl.loop(0, pieces)
     def _(k):
         near_copy(k).wait_send()
-        for group in range(len(groups)):
-            pass_copy(group, k).wait_send()
-        for group in chunks[1]:
-            cross_copy(group, k).wait_send()
+        pass_copy(0, k).wait_send()
+
+    for k in range(pieces + 1):
+        pass_copy(1, k).wait_send()
+        cross_copy(1, k).wait_send()
 
     keep = jnp.where(qa_ref[...] == qb_ref[...], F32(0.0), F32(0.5)).reshape(1, q)
     pltpu.make_async_copy(recv, recv, rr).wait()
@@ -298,7 +310,8 @@
             pltpu.VMEM((4 * block // unit, 2, unit, q), F32),
             pltpu.VMEM((n - 1, rows // unit, 2, unit, q), F32),
             dma, dma((pieces,)), dma((4,)), dma((pieces,)), dma((pieces,)),
-            dma((2, pieces)), dma((2, pieces)), dma((2, pieces)), dma((2, pieces)), dma, dma,
+            dma((2, pieces + 1)), dma((2, pieces + 1)), dma((2, pieces + 1)), dma((2, pieces + 1)),
+            dma, dma,
             pltpu.SemaphoreType.REGULAR, pltpu.SemaphoreType.REGULAR,
         ],
         compiler_params=pltpu.CompilerParams(

time: 51.6 us -> 51.6 us (level)
  no operation moved by 1% of the time
where the time goes in v7:
time: 51.6 us; the launch traced here: 51.4 us
  Pallas kernels  50.8 us (98%)
  local copies, waits for them, and re-layouts  0.65 us (1%)
    pallas_call x1, Pallas kernels, local(): pl.pallas_call(functools.partial(kernel, n), out_shape=jax.ShapeDtypeStru...  50.8 us

profile of v7, /device:TPU:2, one launch (start us, length us, event | category | flops | bytes accessed | tf_op | source)
XLA Modules:
  0.0 51.4 jit_solution(1236030854901729092)
XLA Ops:
  0.0 50.8 %shard_map.64 = f32[2,16,384]{2,1,0:T(8,128)S(1)} custom-call(f32[2,32,7168]{2,1,0:T(8,128)} %a_hbm.1, f32[7168,384]{1,0:T(8,128)} %v_hbm.1, s32[1,7168]{1,0:T(1,128)} %bitcast.4, s32[1,7168]{1,0:T(1,128)} %bitcast.5, s32[384]{0:T(512)} %qa_hbm.1, s32[384]{0:T(512)} %qb_hbm.1), custom_call_target="tpu_custom_call" | custom-call | flops 4227858432 | bytes 12845056 | tf_op jit(solution)/shard_map/pallas_call | solution.py:294
  50.8 0.6 %copy.7 = f32[16,2,384]{2,1,0:T(2,128)} copy(f32[16,2,384]{2,0,1:T(8,128)S(1)} %bitcast.3) | data formatting | bytes 98304 | tf_op jit(solution)/shard_map/transpose | solution.py:326

commit v8 on v6

--- a/solution.py
+++ b/solution.py
@@ -43,8 +43,8 @@
     unit = part.shape[2]
     mine = recv.shape[1]
 
-    first_half = j < 2
-    second_half = j >= 2
+    first_half = j >= 2
+    second_half = j < 2
     barrier = pltpu.get_barrier_semaphore()
     pl.semaphore_signal(barrier, inc=1, device_id={"ab": beside}, device_id_type=MESH)
 

time: 51.6 us -> 52.4 us (1.016)
  no operation moved by 1% of the time
where the time goes in v8:
time: 52.4 us; the launch traced here: 51.8 us
  Pallas kernels  51.1 us (98%)
  local copies, waits for them, and re-layouts  0.65 us (1%)
    pallas_call x1, Pallas kernels, local(): pl.pallas_call(functools.partial(kernel, n), out_shape=jax.ShapeDtypeStru...  51.1 us

profile of v8, /device:TPU:2, one launch (start us, length us, event | category | flops | bytes accessed | tf_op | source)
XLA Modules:
  0.0 51.8 jit_solution(9310150105117285791)
XLA Ops:
  0.0 51.1 %shard_map.64 = f32[2,16,384]{2,1,0:T(8,128)S(1)} custom-call(f32[2,32,7168]{2,1,0:T(8,128)} %a_hbm.1, f32[7168,384]{1,0:T(8,128)} %v_hbm.1, s32[1,7168]{1,0:T(1,128)} %bitcast.4, s32[1,7168]{1,0:T(1,128)} %bitcast.5, s32[384]{0:T(512)} %qa_hbm.1, s32[384]{0:T(512)} %qb_hbm.1), custom_call_target="tpu_custom_call" | custom-call | flops 4227858432 | bytes 12845056 | tf_op jit(solution)/shard_map/pallas_call | solution.py:282
  51.1 0.6 %copy.7 = f32[16,2,384]{2,1,0:T(2,128)} copy(f32[16,2,384]{2,0,1:T(8,128)S(1)} %bitcast.3) | data formatting | bytes 98304 | tf_op jit(solution)/shard_map/transpose | solution.py:313
